TPU v7x, 512 devices: a whole 4x4x16 slice. The times are simulated.
512 devices in a mesh: ref: 32 (over z, core), qry: 16 (over x, y).
Axes of the slice: x: 4, y: 4, z: 16, core: 2. Of those that a mesh axis runs over, the one named last changes fastest.
Arguments:
- queries: bfloat16 [4096, 1024], P('qry'), may hold values from -1 to 1
- ref_panels: bfloat16 [256, 128, 1024], P('ref', 'qry'), may hold values from -1 to 1
- cand_mask: int32 [32, 256], P('qry', 'ref'), may hold values 0 or 1
- panel_time: int32 [256], replicated, may hold values from 0 to 255, as said below
- w_first: float32 [9, 32], replicated, may hold values from -2 to 2
- b_first: float32 [32], replicated, may hold values from -2.5 to 2.5
- w_second: bfloat16 [9, 32], replicated, may hold values from -0.375 to 0.375
Outputs:
- score_map: bfloat16 [4096, 32768], P('qry', 'ref')
Inputs may be any that keep to these rules, and one draw needn't show every extreme that they name: `panel_time`: A permutation of the reference time blocks. The owner of block t is t // 8; every owner has 8 blocks. The 8 panels of one ingest index of ref (panels held by one index) include at most 1 of one owner, and every ingest index has 1 panel of some owner.
All inputs are finite; a program needn't handle non-finite values. No bound on the sum of `cand_mask` on one device may be relied on, other than what follows from the above.
Results may differ from a plain program's by a relative error of at most 0.0059.
Values may be sent and summed in bfloat16 or wider, within the bound.
No kernel may reach another device: no remote copies, remote signals or barrier semaphores. Data moves between devices by JAX's collectives and lax.ppermute only.
A program may use at most 64 MiB of HBM per device.

v0:
```python
import math
import jax
import jax.numpy as jnp
from jax import lax
from jax.sharding import PartitionSpec as P

FRAMES = 256


def with_halo(cells, sides, width):
    for axis, dim in sides:
        count = lax.axis_size(axis)
        ends = count - 1
        head = lax.slice_in_dim(cells, 0, width, axis=dim)
        tail = lax.slice_in_dim(cells, cells.shape[dim] - width, cells.shape[dim], axis=dim)
        cells = jnp.concatenate(
            [
                lax.ppermute(tail, axis, [(i, (i + 1) % count) for i in range(ends)]),
                cells,
                lax.ppermute(head, axis, [((i + 1) % count, i) for i in range(ends)]),
            ],
            axis=dim,
        )
    return cells


def layer_one(strip_cols, w_first, b_first):
    height = strip_cols.shape[0]
    widths = strip_cols.shape[1] - 2
    padded = jnp.pad(strip_cols.astype(jnp.float32), ((1, 1), (0, 0)))
    summed = jnp.broadcast_to(b_first[:, None, None], (b_first.shape[0], height, widths))
    for row_shift in range(3):
        for col_shift in range(3):
            summed = (
                summed
                + w_first[3 * row_shift + col_shift][:, None, None]
                * padded[row_shift : row_shift + height, col_shift : col_shift + widths][None]
            )
    return jnp.maximum(summed, 0.0).astype(jnp.bfloat16)


def layer_two(hidden, w_second):
    height = hidden.shape[1]
    widths = hidden.shape[2] - 2
    padded = jnp.pad(hidden, ((0, 0), (1, 1), (0, 0)))
    summed = jnp.zeros((height, widths), jnp.float32)
    for row_shift in range(3):
        for col_shift in range(3):
            summed = summed + jnp.einsum(
                "c,chw->hw",
                w_second[3 * row_shift + col_shift],
                padded[:, row_shift : row_shift + height, col_shift : col_shift + widths],
                preferred_element_type=jnp.float32,
            )
    return summed


def shards(queries, ref_panels, cand_mask, panel_time, w_first, b_first, w_second):
    owners_count = lax.axis_size("ref")
    my_owner = lax.axis_index("ref")
    blocks_dev = ref_panels.shape[0]
    frames_dev = queries.shape[0]
    videos = frames_dev // FRAMES
    slot_count = max(1, (2 * blocks_dev + owners_count - 1) // owners_count)
    times = panel_time.reshape(owners_count, blocks_dev)
    owner_ids = times // blocks_dev
    within = times % blocks_dev
    earlier = jnp.arange(blocks_dev)[None, :] < jnp.arange(blocks_dev)[:, None]
    same_owner = owner_ids[:, :, None] == owner_ids[:, None, :]
    ranks = jnp.sum((same_owner & earlier[None]).astype(jnp.int32), axis=2)
    owner_mine = lax.dynamic_index_in_dim(owner_ids, my_owner, 0, keepdims=False)
    rank_mine = lax.dynamic_index_in_dim(ranks, my_owner, 0, keepdims=False)
    dest_ids = jnp.arange(owners_count)
    slot_ids = jnp.arange(slot_count)
    select = (
        (owner_mine[None, None, :] == dest_ids[:, None, None])
        & (rank_mine[None, None, :] == slot_ids[None, :, None])
    ).astype(jnp.bfloat16)
    outgoing = jnp.einsum(
        "oki,ird->okrd", select, ref_panels, preferred_element_type=jnp.float32
    ).astype(jnp.bfloat16)
    incoming = lax.all_to_all(outgoing, "ref", split_axis=0, concat_axis=0, tiled=True)
    placing = (
        (owner_ids == my_owner)[None, :, None, :]
        & (ranks[None, :, None, :] == slot_ids[None, None, :, None])
        & (within[None, :, None, :] == jnp.arange(blocks_dev)[:, None, None, None])
    )
    placement = jnp.sum(placing.astype(jnp.int32), axis=3).astype(jnp.bfloat16)
    owned = jnp.einsum(
        "tsk,skrd->trd", placement, incoming, preferred_element_type=jnp.float32
    ).astype(jnp.bfloat16)
    tiles = jnp.einsum(
        "qd,brd->qbr",
        queries,
        lax.all_gather(owned, "qry", axis=1, tiled=True),
        preferred_element_type=jnp.float32,
    ).astype(jnp.bfloat16)
    panel_len = tiles.shape[2]
    ref_cols = blocks_dev * panel_len
    qblock_count = cand_mask.shape[0]
    keeper = cand_mask.astype(jnp.bfloat16)[:, None, :, None]
    sims = (
        tiles.reshape(qblock_count, frames_dev // qblock_count, blocks_dev, panel_len) * keeper
    ).reshape(videos, FRAMES, ref_cols)
    first_layer = jax.vmap(layer_one, in_axes=(0, None, None))
    second_layer = jax.vmap(layer_two, in_axes=(0, None))
    single = with_halo(sims, (("ref", 2),), 1)
    spread = jnp.pad(single, ((0, 0), (0, 0), (1, 1)))
    first_col = first_layer(spread[:, :, 1:4], w_first, b_first)[:, :, :, 0]
    last_col = first_layer(spread[:, :, ref_cols : ref_cols + 3], w_first, b_first)[:, :, :, 0]
    edge_pair = jnp.stack([first_col, last_col])
    near_cols = with_halo(edge_pair, (("ref", 0),), 1)
    left_fill = near_cols[0]
    right_fill = near_cols[3]
    left_use = my_owner >= 0
    right_use = my_owner >= 0
    block_cols = math.gcd(256, ref_cols)
    count = ref_cols // block_cols

    def one_block(block_index):
        strip_cols = lax.dynamic_slice_in_dim(spread, block_index * block_cols, block_cols + 4, 2)
        hidden = first_layer(strip_cols, w_first, b_first)
        first = jnp.where((block_index == 0) & left_use, left_fill, hidden[:, :, :, 0])
        final = jnp.where((block_index == count - 1) & right_use, right_fill, hidden[:, :, :, -1])
        hidden = hidden.at[:, :, :, 0].set(first).at[:, :, :, -1].set(final)
        return second_layer(hidden, w_second).astype(jnp.bfloat16)

    blocks_out = lax.map(one_block, jnp.arange(count, dtype=jnp.int32))
    return jnp.transpose(blocks_out, (1, 2, 0, 3)).reshape(frames_dev, ref_cols)


def solution(mesh):
    placed = (P("qry", None), P("ref", "qry", None), P("qry", "ref"), P(), P(), P(), P())
    return jax.shard_map(
        shards, mesh=mesh, in_specs=placed, out_specs=P("qry", "ref"), check_vma=False
    )
```

profile of v0, /device:TPU:97, one launch (start us, length us, event | category | flops | bytes accessed | tf_op | source)
XLA Modules:
  0.0 401.1 jit_solution(5966374788965295155)
XLA Ops:
  10.3 14.8 %all-to-all-start = ((bf16[32,1,8,1024]{3,2,1,0:T(8,128)(2,1)}), bf16[32,1,8,1024]{3,2,1,0:T(8,128)(2,1)S(1)}, u32[]{:S(2)}, u32[]{:S(2)}) async-start(bf16[32,1,8,1024]{3,2,1,0:T(8,128)(2,1)} %copy.95), calls=%async_computation | async-start | bytes 1048576 | tf_op jit(solution)/shard_map/all_to_all | solution.py:82
  25.2 30.0 %all-to-all-done = bf16[32,1,8,1024]{3,2,1,0:T(8,128)(2,1)S(1)} async-done(((bf16[32,1,8,1024]{3,2,1,0:T(8,128)(2,1)}), bf16[32,1,8,1024]{3,2,1,0:T(8,128)(2,1)S(1)}, u32[]{:S(2)}, u32[]{:S(2)}) %all-to-all-start) | async-done | bytes 524320 | tf_op jit(solution)/shard_map/all_to_all | solution.py:82
  57.5 53.4 %all-gather.2.cloned.1.call-done = bf16[8,128,1024]{2,0,1:T(8,128)(2,1)} async-done(((bf16[8,8,1024]{2,0,1:T(8,128)(2,1)}), bf16[8,128,1024]{2,0,1:T(8,128)(2,1)}) %all-gather.2.cloned.1.call-update) | async-done | bytes 2097168 | tf_op jit(solution)/shard_map/all_gather | solution.py:95
  110.9 4.0 fusion.52
  115.4 5.8 %collective-permute-start = (bf16[1,256,1]{2,1,0:T(8,128)(2,1)S(1)}, bf16[1,256,1]{2,1,0:T(8,128)(2,1)S(1)}, u32[]{:S(2)}, u32[]{:S(2)}) collective-permute-start(bf16[1,256,1]{2,1,0:T(8,128)(2,1)S(1)} %get-tuple-element.254), channel_id=1, source_target_pairs={{0,16},{16,32},{32,48},{48,64},{64,80},{80,96},{96,112},{112,128},... | collective-permute-start | bytes 1544 | tf_op jit(solution)/shard_map/ppermute | solution.py:18
  123.2 4.8 %collective-permute-done.1 = bf16[1,256,1]{2,1,0:T(8,128)(2,1)S(1)} collective-permute-done((bf16[1,256,1]{2,1,0:T(8,128)(2,1)S(1)}, bf16[1,256,1]{2,1,0:T(8,128)(2,1)S(1)}, u32[]{:S(2)}, u32[]{:S(2)}) %collective-permute-start.1) | collective-permute-done | bytes 544 | tf_op jit(solution)/shard_map/ppermute | solution.py:20
  132.8 4.9 %collective-permute-start.2 = (bf16[1,1,32,256]{3,2,1,0:T(8,128)(2,1)S(1)}, bf16[1,1,32,256]{3,2,1,0:T(8,128)(2,1)}, u32[]{:S(2)}, u32[]{:S(2)}) collective-permute-start(bf16[1,1,32,256]{3,2,1,0:T(8,128)(2,1)S(1)} %maximum_convert_fusion.2), channel_id=1, source_target_pairs={{0,16},{16,32},{32,48},{48,64},{64,80},{80,96},{96,112},{112,128},... | collective-permute-start | bytes 49160 | tf_op jit(solution)/shard_map/ppermute | solution.py:18
  140.0 251.9 %while.15 = (s32[]{:T(128)}, bf16[4,1,256,256]{3,2,1,0:T(8,128)(2,1)}, f32[32]{0:T(128)}, f32[9,32]{1,0:T(8,128)S(1)}, s32[4]{0:T(128)}, /*index=5*/bf16[1,256,1...) while((s32[]{:T(128)}, ...), condition=%wide.region_3.4_spmd, body=%wide.region_2.3_spmd.sunk | while | flops 80692224 | bytes 88695848 | solution.py:128
  149.3 14.2 %maximum_convert_fusion.4 = bf16[1,32,256,258]{2,1,3,0:T(8,128)(2,1)S(1)} fusion(f32[256,258]{0,1:T(8,128)S(1)} %copy.138, f32[32]{0:T(128)S(1)} %get-tuple-element.355, f32[256,258]{0,1:T(8,128)} %copy.139, f32[32]{0:T(128)S(1)} %get-tuple-element.357, f32[256,258]{0,1:T(8,128)} %copy.140, f32[32]{0:T(128)S(1)} %get-tuple-element.359, ...), kind=kLoop, calls=%fused_computation.clone.1 | loop fusion | flops 42270720 | bytes 6606080 | tf_op jit(solution)/shard_map/while/body/eval_jaxpr/vmap()/convert_element_type | solution.py:39
  174.5 3.6 fusion.119
  178.2 3.6 fusion.120
  190.9 3.6 fusion.124
  194.7 3.6 fusion.125
  198.4 3.6 fusion.126
  212.3 14.2 %maximum_convert_fusion.4 = bf16[1,32,256,258]{2,1,3,0:T(8,128)(2,1)S(1)} fusion(f32[256,258]{0,1:T(8,128)S(1)} %copy.138, f32[32]{0:T(128)S(1)} %get-tuple-element.355, f32[256,258]{0,1:T(8,128)} %copy.139, f32[32]{0:T(128)S(1)} %get-tuple-element.357, f32[256,258]{0,1:T(8,128)} %copy.140, f32[32]{0:T(128)S(1)} %get-tuple-element.359, ...), kind=kLoop, calls=%fused_computation.clone.1 | loop fusion | flops 42270720 | bytes 6606080 | tf_op jit(solution)/shard_map/while/body/eval_jaxpr/vmap()/convert_element_type | solution.py:39
  237.5 3.6 fusion.119
  241.2 3.6 fusion.120
  253.9 3.6 fusion.124
  257.7 3.6 fusion.125
  261.4 3.6 fusion.126
  275.2 14.2 %maximum_convert_fusion.4 = bf16[1,32,256,258]{2,1,3,0:T(8,128)(2,1)S(1)} fusion(f32[256,258]{0,1:T(8,128)S(1)} %copy.138, f32[32]{0:T(128)S(1)} %get-tuple-element.355, f32[256,258]{0,1:T(8,128)} %copy.139, f32[32]{0:T(128)S(1)} %get-tuple-element.357, f32[256,258]{0,1:T(8,128)} %copy.140, f32[32]{0:T(128)S(1)} %get-tuple-element.359, ...), kind=kLoop, calls=%fused_computation.clone.1 | loop fusion | flops 42270720 | bytes 6606080 | tf_op jit(solution)/shard_map/while/body/eval_jaxpr/vmap()/convert_element_type | solution.py:39
  300.5 3.6 fusion.119
  304.2 3.6 fusion.120
  316.9 3.6 fusion.124
  320.7 3.6 fusion.125
  324.4 3.6 fusion.126
  338.2 14.2 %maximum_convert_fusion.4 = bf16[1,32,256,258]{2,1,3,0:T(8,128)(2,1)S(1)} fusion(f32[256,258]{0,1:T(8,128)S(1)} %copy.138, f32[32]{0:T(128)S(1)} %get-tuple-element.355, f32[256,258]{0,1:T(8,128)} %copy.139, f32[32]{0:T(128)S(1)} %get-tuple-element.357, f32[256,258]{0,1:T(8,128)} %copy.140, f32[32]{0:T(128)S(1)} %get-tuple-element.359, ...), kind=kLoop, calls=%fused_computation.clone.1 | loop fusion | flops 42270720 | bytes 6606080 | tf_op jit(solution)/shard_map/while/body/eval_jaxpr/vmap()/convert_element_type | solution.py:39
  363.5 3.6 fusion.119
  367.2 3.6 fusion.120
  379.9 3.6 fusion.124
  383.6 3.6 fusion.125
  387.4 3.6 fusion.126
  (176 shorter events, 132.4 us)
Async XLA Ops:
  6.5 104.4 %copy-start = (bf16[256,1024]{1,0:T(8,128)(2,1)S(1)}, bf16[256,1024]{1,0:T(8,128)(2,1)}, u32[]{:S(2)}) copy-start(bf16[256,1024]{1,0:T(8,128)(2,1)} %param.13) | copy-start | bytes 1572868
  10.3 44.8 %all-to-all-start = ((bf16[32,1,8,1024]{3,2,1,0:T(8,128)(2,1)}), bf16[32,1,8,1024]{3,2,1,0:T(8,128)(2,1)S(1)}, u32[]{:S(2)}, u32[]{:S(2)}) async-start(bf16[32,1,8,1024]{3,2,1,0:T(8,128)(2,1)} %copy.95), calls=%async_computation | async-start | bytes 1048576 | tf_op jit(solution)/shard_map/all_to_all | solution.py:82
  25.1 85.8 %all-gather.2.cloned.1.call-start = ((), (), s32[]{:S(2)}) async-start(), calls=%async_computation.1 | async-start | bytes 2228224 | tf_op jit(solution)/shard_map/all_gather | solution.py:95
  57.3 65.9 %copy-start.2 = (f32[9,32]{1,0:T(8,128)S(1)}, f32[9,32]{1,0:T(8,128)}, u32[]{:S(2)}) copy-start(f32[9,32]{1,0:T(8,128)} %param.17) | copy-start | bytes 3460
  115.4 7.7 %collective-permute-start = (bf16[1,256,1]{2,1,0:T(8,128)(2,1)S(1)}, bf16[1,256,1]{2,1,0:T(8,128)(2,1)S(1)}, u32[]{:S(2)}, u32[]{:S(2)}) collective-permute-start(bf16[1,256,1]{2,1,0:T(8,128)(2,1)S(1)} %get-tuple-element.254), channel_id=1, source_target_pairs={{0,16},{16,32},{32,48},{48,64},{64,80},{80,96},{96,112},{112,128},... | collective-permute-start | bytes 1544 | tf_op jit(solution)/shard_map/ppermute | solution.py:18
  121.2 6.8 %collective-permute-start.1 = (bf16[1,256,1]{2,1,0:T(8,128)(2,1)S(1)}, bf16[1,256,1]{2,1,0:T(8,128)(2,1)S(1)}, u32[]{:S(2)}, u32[]{:S(2)}) collective-permute-start(bf16[1,256,1]{2,1,0:T(8,128)(2,1)S(1)} %get-tuple-element.253), channel_id=1, source_target_pairs={{16,0},{32,16},{48,32},{64,48},{80,64},{96,80},{112,96},{128,112},... | collective-permute-start | bytes 1544 | tf_op jit(solution)/shard_map/ppermute | solution.py:20
  130.1 9.3 %collective-permute-start.3 = (bf16[1,1,32,256]{3,2,1,0:T(8,128)(2,1)S(1)}, bf16[1,1,32,256]{3,2,1,0:T(8,128)(2,1)}, u32[]{:S(2)}, u32[]{:S(2)}) collective-permute-start(bf16[1,1,32,256]{3,2,1,0:T(8,128)(2,1)S(1)} %maximum_convert_fusion.1), channel_id=1, source_target_pairs={{16,0},{32,16},{48,32},{64,48},{80,64},{96,80},{112,96},{128,112},... | collective-permute-start | bytes 49160 | tf_op jit(solution)/shard_map/ppermute | solution.py:20
  132.8 6.6 %collective-permute-start.2 = (bf16[1,1,32,256]{3,2,1,0:T(8,128)(2,1)S(1)}, bf16[1,1,32,256]{3,2,1,0:T(8,128)(2,1)}, u32[]{:S(2)}, u32[]{:S(2)}) collective-permute-start(bf16[1,1,32,256]{3,2,1,0:T(8,128)(2,1)S(1)} %maximum_convert_fusion.2), channel_id=1, source_target_pairs={{0,16},{16,32},{32,48},{48,64},{64,80},{80,96},{96,112},{112,128},... | collective-permute-start | bytes 49160 | tf_op jit(solution)/shard_map/ppermute | solution.py:18
  163.5 3.2 copy-start.1
  163.5 7.3 %copy-start.3 = (bf16[9,32]{1,0:T(8,128)(2,1)S(1)}, bf16[9,32]{1,0:T(8,128)(2,1)}, u32[]{:S(2)}) copy-start(bf16[9,32]{1,0:T(8,128)(2,1)} %get-tuple-element.413) | copy-start | bytes 1732 | tf_op jit(solution)/shard_map/while
  226.5 3.2 copy-start.1
  226.5 7.3 %copy-start.3 = (bf16[9,32]{1,0:T(8,128)(2,1)S(1)}, bf16[9,32]{1,0:T(8,128)(2,1)}, u32[]{:S(2)}) copy-start(bf16[9,32]{1,0:T(8,128)(2,1)} %get-tuple-element.413) | copy-start | bytes 1732 | tf_op jit(solution)/shard_map/while
  289.5 3.2 copy-start.1
  289.5 7.3 %copy-start.3 = (bf16[9,32]{1,0:T(8,128)(2,1)S(1)}, bf16[9,32]{1,0:T(8,128)(2,1)}, u32[]{:S(2)}) copy-start(bf16[9,32]{1,0:T(8,128)(2,1)} %get-tuple-element.413) | copy-start | bytes 1732 | tf_op jit(solution)/shard_map/while
  352.4 3.2 copy-start.1
  352.5 7.3 %copy-start.3 = (bf16[9,32]{1,0:T(8,128)(2,1)S(1)}, bf16[9,32]{1,0:T(8,128)(2,1)}, u32[]{:S(2)}) copy-start(bf16[9,32]{1,0:T(8,128)(2,1)} %get-tuple-element.413) | copy-start | bytes 1732 | tf_op jit(solution)/shard_map/while
Sparse Core Ops, SparseCore 0:
  56.6 54.2 all-gather.1
where the time goes:
time: 404 us; the launch traced here: 401 us
  matrix products  127 us (31%)
  waiting for transfers between devices  88.2 us (22%)
  other arithmetic  78.1 us (19%)
  local copies, waits for them, and re-layouts  56.3 us (14%)
  starting transfers between devices  29.3 us (7%)
  between operations  13.6 us (3%)
  loops' own time  8.92 us (2%)
    dot_general x36, matrix products, layer_two(): jnp.einsum('c,chw->hw', w_second[3 * row_shift + col_shift], padded[:, ro...  120 us
    convert_element_type x6, other arithmetic, layer_one(): return jnp.maximum(summed, 0.0).astype(jnp.bfloat16)  58.4 us
    all_gather x1, waiting for transfers between devices, shards(): lax.all_gather(owned, 'qry', axis=1, tiled=True)  53.4 us
    all_to_all x1, waiting for transfers between devices, shards(): lax.all_to_all(outgoing, 'ref', split_axis=0, concat_axis=0, tiled=True)  30 us
    mul x44, local copies, waits for them, and re-layouts, layer_one(): w_first[3 * row_shift + col_shift][:, None, None]  24.6 us
    all_to_all x1, starting transfers between devices, shards(): lax.all_to_all(outgoing, 'ref', split_axis=0, concat_axis=0, tiled=True)  14.8 us
    while x20, local copies, waits for them, and re-layouts  12.8 us
    scatter x8, other arithmetic, one_block(): hidden = hidden.at[:, :, :, 0].set(first).at[:, :, :, -1].set(final)  10.9 us
  transfers between devices with their start and end apart: 6, of which 3 were waited for; matrix products, arithmetic and copies ran while one was open for 1% of the time, Pallas kernels for 0%

commit v1 on v0

--- a/solution.py
+++ b/solution.py
@@ -92,7 +92,9 @@
     tiles = jnp.einsum(
         "qd,brd->qbr",
         queries,
-        lax.all_gather(owned, "qry", axis=1, tiled=True),
+        jnp.concatenate(
+            lax.all_to_all(jnp.stack([owned] * lax.axis_size("qry")), "qry", 0, 0), axis=1
+        ),
         preferred_element_type=jnp.float32,
     ).astype(jnp.bfloat16)
     panel_len = tiles.shape[2]

time: 404 us -> 371 us (0.918)
  the two profiles are of different devices: /device:TPU:97 before, /device:TPU:1 now
where the time goes in v1:
time: 371 us; the launch traced here: 368 us
  matrix products  124 us (33%)
  other arithmetic  77.4 us (21%)
  waiting for transfers between devices  64.5 us (17%)
  local copies, waits for them, and re-layouts  57.9 us (16%)
  starting transfers between devices  35 us (9%)
  loops' own time  8.92 us (2%)
    dot_general x36, matrix products, layer_two(): jnp.einsum('c,chw->hw', w_second[3 * row_shift + col_shift], padded[:, ro...  120 us
    convert_element_type x6, other arithmetic, layer_one(): return jnp.maximum(summed, 0.0).astype(jnp.bfloat16)  58.4 us
    all_to_all x1, waiting for transfers between devices, shards(): lax.all_to_all(outgoing, 'ref', split_axis=0, concat_axis=0, tiled=True)  33.5 us
    all_to_all x1, waiting for transfers between devices, shards(): lax.all_to_all(jnp.stack([owned] * lax.axis_size('qry')), 'qry', 0, 0)  28.7 us
    mul x44, local copies, waits for them, and re-layouts, layer_one(): w_first[3 * row_shift + col_shift][:, None, None]  24.6 us
    all_to_all x1, starting transfers between devices, shards(): lax.all_to_all(outgoing, 'ref', split_axis=0, concat_axis=0, tiled=True)  16.9 us
    while x20, local copies, waits for them, and re-layouts  12.8 us
    scatter x8, other arithmetic, one_block(): hidden = hidden.at[:, :, :, 0].set(first).at[:, :, :, -1].set(final)  10.9 us
  transfers between devices with their start and end apart: 6, of which 3 were waited for; matrix products, arithmetic and copies ran while one was open for 1% of the time, Pallas kernels for 0%

profile of v1, /device:TPU:1, one launch (start us, length us, event | category | flops | bytes accessed | tf_op | source)
XLA Modules:
  0.0 368.3 jit_solution(2649008010921877142)
XLA Ops:
  3.8 16.9 %all-to-all-start = ((bf16[32,1,8,1024]{3,2,1,0:T(8,128)(2,1)}), bf16[32,1,8,1024]{3,2,1,0:T(8,128)(2,1)S(1)}, u32[]{:S(2)}, u32[]{:S(2)}) async-start(bf16[32,1,8,1024]{3,2,1,0:T(8,128)(2,1)} %copy.84), calls=%async_computation | async-start | bytes 1048576 | tf_op jit(solution)/shard_map/all_to_all | solution.py:82
  20.7 33.5 %all-to-all-done = bf16[32,1,8,1024]{3,2,1,0:T(8,128)(2,1)S(1)} async-done(((bf16[32,1,8,1024]{3,2,1,0:T(8,128)(2,1)}), bf16[32,1,8,1024]{3,2,1,0:T(8,128)(2,1)S(1)}, u32[]{:S(2)}, u32[]{:S(2)}) %all-to-all-start) | async-done | bytes 524320 | tf_op jit(solution)/shard_map/all_to_all | solution.py:82
  56.5 6.8 %all-to-all-start.1 = ((bf16[16,8,8,1024]{3,2,1,0:T(8,128)(2,1)}), bf16[16,8,8,1024]{3,2,1,0:T(8,128)(2,1)}, u32[]{:S(2)}, u32[]{:S(2)}) async-start(bf16[16,8,8,1024]{3,2,1,0:T(8,128)(2,1)} %stack.2), calls=%async_computation.1 | async-start | bytes 4194304 | tf_op jit(solution)/shard_map/all_to_all | solution.py:96
  63.7 28.7 %all-to-all-done.1 = bf16[16,8,8,1024]{3,2,1,0:T(8,128)(2,1)} async-done(((bf16[16,8,8,1024]{3,2,1,0:T(8,128)(2,1)}), bf16[16,8,8,1024]{3,2,1,0:T(8,128)(2,1)}, u32[]{:S(2)}, u32[]{:S(2)}) %all-to-all-start.1) | async-done | bytes 2097184 | tf_op jit(solution)/shard_map/all_to_all | solution.py:96
  108.1 3.6 collective-permute-start.2
  114.1 251.9 %while.15 = (s32[]{:T(128)}, bf16[4,1,256,256]{3,2,1,0:T(8,128)(2,1)}, f32[32]{0:T(128)}, f32[9,32]{1,0:T(8,128)S(1)}, s32[4]{0:T(128)}, /*index=5*/bf16[1,256,1...) while((s32[]{:T(128)}, ...), condition=%wide.region_3.4_spmd, body=%wide.region_2.3_spmd.sunk | while | flops 80692224 | bytes 88695848 | solution.py:130
  123.3 14.2 %maximum_convert_fusion.4 = bf16[1,32,256,258]{2,1,3,0:T(8,128)(2,1)S(1)} fusion(f32[256,258]{0,1:T(8,128)S(1)} %copy.130, f32[32]{0:T(128)S(1)} %get-tuple-element.355, f32[256,258]{0,1:T(8,128)} %copy.131, f32[32]{0:T(128)S(1)} %get-tuple-element.357, f32[256,258]{0,1:T(8,128)} %copy.132, f32[32]{0:T(128)S(1)} %get-tuple-element.359, ...), kind=kLoop, calls=%fused_computation.clone.1 | loop fusion | flops 42270720 | bytes 6606080 | tf_op jit(solution)/shard_map/while/body/eval_jaxpr/vmap()/convert_element_type | solution.py:39
  144.9 3.6 fusion.120
  148.6 3.6 fusion.121
  152.3 3.6 fusion.122
  165.0 3.6 fusion.126
  168.8 3.6 fusion.127
  172.5 3.6 fusion.128
  186.3 14.2 %maximum_convert_fusion.4 = bf16[1,32,256,258]{2,1,3,0:T(8,128)(2,1)S(1)} fusion(f32[256,258]{0,1:T(8,128)S(1)} %copy.130, f32[32]{0:T(128)S(1)} %get-tuple-element.355, f32[256,258]{0,1:T(8,128)} %copy.131, f32[32]{0:T(128)S(1)} %get-tuple-element.357, f32[256,258]{0,1:T(8,128)} %copy.132, f32[32]{0:T(128)S(1)} %get-tuple-element.359, ...), kind=kLoop, calls=%fused_computation.clone.1 | loop fusion | flops 42270720 | bytes 6606080 | tf_op jit(solution)/shard_map/while/body/eval_jaxpr/vmap()/convert_element_type | solution.py:39
  211.6 3.6 fusion.121
  215.3 3.6 fusion.122
  228.0 3.6 fusion.126
  231.7 3.6 fusion.127
  235.5 3.6 fusion.128
  249.3 14.2 %maximum_convert_fusion.4 = bf16[1,32,256,258]{2,1,3,0:T(8,128)(2,1)S(1)} fusion(f32[256,258]{0,1:T(8,128)S(1)} %copy.130, f32[32]{0:T(128)S(1)} %get-tuple-element.355, f32[256,258]{0,1:T(8,128)} %copy.131, f32[32]{0:T(128)S(1)} %get-tuple-element.357, f32[256,258]{0,1:T(8,128)} %copy.132, f32[32]{0:T(128)S(1)} %get-tuple-element.359, ...), kind=kLoop, calls=%fused_computation.clone.1 | loop fusion | flops 42270720 | bytes 6606080 | tf_op jit(solution)/shard_map/while/body/eval_jaxpr/vmap()/convert_element_type | solution.py:39
  270.9 3.6 fusion.120
  274.6 3.6 fusion.121
  278.3 3.6 fusion.122
  291.0 3.6 fusion.126
  294.7 3.6 fusion.127
  298.5 3.6 fusion.128
  312.3 14.2 %maximum_convert_fusion.4 = bf16[1,32,256,258]{2,1,3,0:T(8,128)(2,1)S(1)} fusion(f32[256,258]{0,1:T(8,128)S(1)} %copy.130, f32[32]{0:T(128)S(1)} %get-tuple-element.355, f32[256,258]{0,1:T(8,128)} %copy.131, f32[32]{0:T(128)S(1)} %get-tuple-element.357, f32[256,258]{0,1:T(8,128)} %copy.132, f32[32]{0:T(128)S(1)} %get-tuple-element.359, ...), kind=kLoop, calls=%fused_computation.clone.1 | loop fusion | flops 42270720 | bytes 6606080 | tf_op jit(solution)/shard_map/while/body/eval_jaxpr/vmap()/convert_element_type | solution.py:39
  337.5 3.6 fusion.121
  341.3 3.6 fusion.122
  354.0 3.6 fusion.126
  357.7 3.6 fusion.127
  361.4 3.6 fusion.128
  (179 shorter events, 133.9 us)
Async XLA Ops:
  0.0 92.4 %copy-start = (bf16[256,1024]{1,0:T(8,128)(2,1)S(1)}, bf16[256,1024]{1,0:T(8,128)(2,1)}, u32[]{:S(2)}) copy-start(bf16[256,1024]{1,0:T(8,128)(2,1)} %param.13) | copy-start | bytes 1572868
  3.8 59.5 %copy-start.4 = (s32[2,8]{1,0:T(2,128)S(1)}, s32[2,8]{1,0:T(2,128)}, u32[]{:S(2)}) copy-start(s32[2,8]{1,0:T(2,128)} %param.15) | copy-start | bytes 196
  3.8 50.4 %all-to-all-start = ((bf16[32,1,8,1024]{3,2,1,0:T(8,128)(2,1)}), bf16[32,1,8,1024]{3,2,1,0:T(8,128)(2,1)S(1)}, u32[]{:S(2)}, u32[]{:S(2)}) async-start(bf16[32,1,8,1024]{3,2,1,0:T(8,128)(2,1)} %copy.84), calls=%async_computation | async-start | bytes 1048576 | tf_op jit(solution)/shard_map/all_to_all | solution.py:82
  56.5 35.9 %all-to-all-start.1 = ((bf16[16,8,8,1024]{3,2,1,0:T(8,128)(2,1)}), bf16[16,8,8,1024]{3,2,1,0:T(8,128)(2,1)}, u32[]{:S(2)}, u32[]{:S(2)}) async-start(bf16[16,8,8,1024]{3,2,1,0:T(8,128)(2,1)} %stack.2), calls=%async_computation.1 | async-start | bytes 4194304 | tf_op jit(solution)/shard_map/all_to_all | solution.py:96
  63.5 37.5 %copy-start.2 = (f32[9,32]{1,0:T(8,128)S(1)}, f32[9,32]{1,0:T(8,128)}, u32[]{:S(2)}) copy-start(f32[9,32]{1,0:T(8,128)} %param.17) | copy-start | bytes 3460
  95.2 5.8 %collective-permute-start = (bf16[1,256,1]{2,1,0:T(8,128)(2,1)S(1)}, bf16[1,256,1]{2,1,0:T(8,128)(2,1)S(1)}, u32[]{:S(2)}, u32[]{:S(2)}) collective-permute-start(bf16[1,256,1]{2,1,0:T(8,128)(2,1)S(1)} %get-tuple-element.254), channel_id=1, source_target_pairs={{0,16},{16,32},{32,48},{48,64},{64,80},{80,96},{96,112},{112,128},... | collective-permute-start | bytes 1544 | tf_op jit(solution)/shard_map/ppermute | solution.py:18
  97.7 5.6 %collective-permute-start.1 = (bf16[1,256,1]{2,1,0:T(8,128)(2,1)S(1)}, bf16[1,256,1]{2,1,0:T(8,128)(2,1)S(1)}, u32[]{:S(2)}, u32[]{:S(2)}) collective-permute-start(bf16[1,256,1]{2,1,0:T(8,128)(2,1)S(1)} %get-tuple-element.253), channel_id=1, source_target_pairs={{16,0},{32,16},{48,32},{64,48},{80,64},{96,80},{112,96},{128,112},... | collective-permute-start | bytes 1544 | tf_op jit(solution)/shard_map/ppermute | solution.py:20
  105.4 8.1 %collective-permute-start.3 = (bf16[1,1,32,256]{3,2,1,0:T(8,128)(2,1)S(1)}, bf16[1,1,32,256]{3,2,1,0:T(8,128)(2,1)}, u32[]{:S(2)}, u32[]{:S(2)}) collective-permute-start(bf16[1,1,32,256]{3,2,1,0:T(8,128)(2,1)S(1)} %maximum_convert_fusion.1), channel_id=1, source_target_pairs={{16,0},{32,16},{48,32},{64,48},{80,64},{96,80},{112,96},{128,112},... | collective-permute-start | bytes 49160 | tf_op jit(solution)/shard_map/ppermute | solution.py:20
  108.1 5.4 %collective-permute-start.2 = (bf16[1,1,32,256]{3,2,1,0:T(8,128)(2,1)S(1)}, bf16[1,1,32,256]{3,2,1,0:T(8,128)(2,1)}, u32[]{:S(2)}, u32[]{:S(2)}) collective-permute-start(bf16[1,1,32,256]{3,2,1,0:T(8,128)(2,1)S(1)} %maximum_convert_fusion.2), channel_id=1, source_target_pairs={{0,16},{16,32},{32,48},{48,64},{64,80},{80,96},{96,112},{112,128},... | collective-permute-start | bytes 49160 | tf_op jit(solution)/shard_map/ppermute | solution.py:18
  137.6 3.2 copy-start.1
  137.6 7.3 %copy-start.3 = (bf16[9,32]{1,0:T(8,128)(2,1)S(1)}, bf16[9,32]{1,0:T(8,128)(2,1)}, u32[]{:S(2)}) copy-start(bf16[9,32]{1,0:T(8,128)(2,1)} %get-tuple-element.413) | copy-start | bytes 1732 | tf_op jit(solution)/shard_map/while
  200.6 3.2 copy-start.1
  200.6 7.3 %copy-start.3 = (bf16[9,32]{1,0:T(8,128)(2,1)S(1)}, bf16[9,32]{1,0:T(8,128)(2,1)}, u32[]{:S(2)}) copy-start(bf16[9,32]{1,0:T(8,128)(2,1)} %get-tuple-element.413) | copy-start | bytes 1732 | tf_op jit(solution)/shard_map/while
  263.6 3.2 copy-start.1
  263.6 7.3 %copy-start.3 = (bf16[9,32]{1,0:T(8,128)(2,1)S(1)}, bf16[9,32]{1,0:T(8,128)(2,1)}, u32[]{:S(2)}) copy-start(bf16[9,32]{1,0:T(8,128)(2,1)} %get-tuple-element.413) | copy-start | bytes 1732 | tf_op jit(solution)/shard_map/while
  326.5 3.2 copy-start.1
  326.5 7.3 %copy-start.3 = (bf16[9,32]{1,0:T(8,128)(2,1)S(1)}, bf16[9,32]{1,0:T(8,128)(2,1)}, u32[]{:S(2)}) copy-start(bf16[9,32]{1,0:T(8,128)(2,1)} %get-tuple-element.413) | copy-start | bytes 1732 | tf_op jit(solution)/shard_map/while
